TPU v7x, 32 devices: a whole 2x2x4 slice. The times are simulated.
32 devices in a mesh: row: 4 (over z), col: 8 (over y, x, core).
Axes of the slice: x: 2, y: 2, z: 4, core: 2. Of those that a mesh axis runs over, the one named last changes fastest.
Arguments:
- tokens: bfloat16 [512, 6144], P('row', 'col'), may hold values from -6 to 6
- weight: bfloat16 [6144, 24576], P('row', 'col'), may hold values from -0.078125 to 0.078125
- act_grad: bfloat16 [512, 24576], P('row', 'col'), may hold values from -6 to 6
Outputs:
- activation: bfloat16 [512, 24576], P('row', 'col')
- input_grad: bfloat16 [512, 6144], P('col', 'row')
- weight_grad: bfloat16 [6144, 24576], P('row', 'col')
All inputs are finite; a program needn't handle non-finite values.
Results may differ from a plain program's by a relative error of at most 0.014.
Values may be sent and summed in bfloat16 or wider, within the bound.
A program may use at most 128 MiB of HBM per device.

v0:
```python
import jax
import jax.numpy as jnp
from jax import lax
from jax.sharding import PartitionSpec as P

root_two_pi = 0.7978845608028654
cubic_coef = 0.044715


def gelu_tanh(value):
    return (
        0.5 * value * (1.0 + jnp.tanh(root_two_pi * (value + cubic_coef * value * value * value)))
    )


def gelu_slope(value):
    angle = jnp.tanh(root_two_pi * (value + cubic_coef * value * value * value))
    return 0.5 * (1.0 + angle) + 0.5 * value * (1.0 - angle * angle) * root_two_pi * (
        1.0 + 3.0 * cubic_coef * value * value
    )


def local(tokens, weight, act_grad):
    row_block = lax.all_gather(tokens, "col", axis=1, tiled=True)
    hidden_pre = jnp.dot(
        row_block,
        lax.all_gather(weight, "row", axis=0, tiled=True),
        preferred_element_type=jnp.float32,
    )
    activation = gelu_tanh(hidden_pre).astype(jnp.bfloat16)
    hidden_grad = (act_grad.astype(jnp.float32) * gelu_slope(hidden_pre)).astype(jnp.bfloat16)
    all_hidden = lax.all_gather(hidden_grad, "row", axis=0, tiled=True)
    token_cols = lax.all_to_all(row_block, "row", split_axis=1, concat_axis=0, tiled=True)
    weight_grad = lax.dot_general(
        token_cols, all_hidden, (((0,), (0,)), ((), ())), preferred_element_type=jnp.float32
    ).astype(jnp.bfloat16)
    input_grad = lax.psum_scatter(
        lax.dot_general(
            all_hidden, weight, (((1,), (1,)), ((), ())), preferred_element_type=jnp.float32
        ).astype(jnp.bfloat16),
        "col",
        scatter_dimension=0,
        tiled=True,
    )
    return (activation, input_grad, weight_grad)


def solution(mesh):
    placed = (P("row", "col"), P("row", "col"), P("row", "col"))
    return jax.shard_map(
        local,
        mesh=mesh,
        in_specs=placed,
        out_specs=(P("row", "col"), P("col", "row"), P("row", "col")),
        check_vma=False,
    )
```

profile of v0, /device:TPU:7, one launch (start us, length us, event | category | flops | bytes accessed | tf_op | source)
XLA Modules:
  0.0 832.3 jit_solution(6804147504080113754)
XLA Ops:
  7.2 0.0 all-gather.4.cloned.1.call-start
  7.2 1.7 copy.8
  9.0 0.0 all-gather.4.cloned.1.call-update
  9.0 0.0 copy-start
  9.0 0.0 all-gather.6.cloned.1.call-start
  9.0 0.7 all-gather.6.cloned.1.call-update
  9.7 0.0 all-gather.8.cloned.1.call-start
  9.8 27.1 %all-gather.4.cloned.1.call-done = bf16[128,6144]{0,1:T(8,128)(2,1)} async-done(((bf16[128,768]{0,1:T(8,128)(2,1)}), bf16[128,6144]{0,1:T(8,128)(2,1)}) %all-gather.4.cloned.1.call-update) | async-done | bytes 1572880 | tf_op jit(solution)/shard_map/all_gather | solution.py:24
  36.9 633.6 %all-gather.6.cloned.1.call-done = bf16[6144,3072]{1,0:T(8,128)(2,1)} async-done(((bf16[1536,3072]{1,0:T(8,128)(2,1)}), bf16[6144,3072]{1,0:T(8,128)(2,1)}) %all-gather.6.cloned.1.call-update) | async-done | bytes 37748752 | tf_op jit(solution)/shard_map/all_gather | solution.py:27
  670.5 0.0 copy-done
  670.5 16.5 %fusion.7 = (bf16[128,3072]{1,0:T(8,128)(2,1)}, bf16[128,3072]{1,0:T(8,128)(2,1)}) fusion(bf16[128,3072]{1,0:T(8,128)(2,1)S(1)} %copy-done, bf16[128,6144]{0,1:T(8,128)(2,1)} %all-gather.4.cloned.1.call-done, bf16[6144,3072]{1,0:T(8,128)(2,1)} %all-gather.6.cloned.1.call-done), kind=kOutput, calls=%fused_computation.11 | convolution fusion | flops 4840488960 | bytes 41680896 | tf_op jit(solution)/shard_map/dot_general | solution.py:25
  686.9 0.0 all-gather.8.cloned.1.call-update
  687.0 3.6 all-to-all-start
  690.6 0.0 reduce-scatter.2.cloned.1.call-start
  690.6 88.3 %all-gather.8.cloned.1.call-done = bf16[512,3072]{1,0:T(8,128)(2,1)} async-done(((bf16[128,3072]{1,0:T(8,128)(2,1)}), bf16[512,3072]{1,0:T(8,128)(2,1)}) %all-gather.8.cloned.1.call-update) | async-done | bytes 3145744 | tf_op jit(solution)/shard_map/all_gather | solution.py:32
  778.9 10.3 %convolution_convert_fusion.1 = bf16[512,1536]{1,0:T(8,128)(2,1)} fusion(bf16[512,3072]{1,0:T(8,128)(2,1)} %all-gather.8.cloned.1.call-done, bf16[1536,3072]{1,0:T(8,128)(2,1)} %param.4), kind=kOutput, calls=%fused_computation.2 | convolution fusion | flops 4832624640 | bytes 14155776 | tf_op jit(solution)/shard_map/dot_general | solution.py:38
  789.2 0.0 reduce-scatter.2.cloned.1.call-update
  789.3 0.0 all-to-all-done
  789.3 0.7 copy.9
  790.0 9.6 %fusion = bf16[1536,3072]{0,1:T(8,128)(2,1)} fusion(bf16[512,3072]{1,0:T(8,128)(2,1)} %all-gather.8.cloned.1.call-done, bf16[512,1536]{1,0:T(8,128)(2,1)S(1)} %bitcast.12), kind=kOutput, calls=%fused_computation.1 | convolution fusion | flops 4836556800 | bytes 14155776 | tf_op jit(solution)/shard_map/dot_general | solution.py:34
  799.6 12.6 %copy.10 = bf16[1536,3072]{1,0:T(8,128)(2,1)} copy(bf16[1536,3072]{0,1:T(8,128)(2,1)} %fusion) | data formatting | bytes 18874368
  812.2 13.6 %reduce-scatter.2.cloned.1.call-done = bf16[64,1536]{1,0:T(8,128)(2,1)} async-done(((bf16[512,1536]{1,0:T(8,128)(2,1)}), bf16[64,1536]{1,0:T(8,128)(2,1)}) %reduce-scatter.2.cloned.1.call-update) | async-done | bytes 196624 | tf_op jit(solution)/shard_map/reduce_scatter | solution.py:37
Async XLA Ops:
  7.2 29.7 %all-gather.4.cloned.1.call-start = ((), (), s32[]{:S(2)}) async-start(), calls=%async_computation.2 | async-start | bytes 1769472 | tf_op jit(solution)/shard_map/all_gather | solution.py:24
  9.0 661.5 %copy-start = (bf16[128,3072]{1,0:T(8,128)(2,1)S(1)}, bf16[128,3072]{1,0:T(8,128)(2,1)}, u32[]{:S(2)}) copy-start(bf16[128,3072]{1,0:T(8,128)(2,1)} %param.5) | copy-start | bytes 2359300
  9.0 661.5 %all-gather.6.cloned.1.call-start = ((), (), s32[]{:S(2)}) async-start(), calls=%async_computation.3 | async-start | bytes 47185920 | tf_op jit(solution)/shard_map/all_gather | solution.py:27
  9.7 769.1 %all-gather.8.cloned.1.call-start = ((), (), s32[]{:S(2)}) async-start(), calls=%async_computation.4 | async-start | bytes 3932160 | tf_op jit(solution)/shard_map/all_gather | solution.py:32
  687.0 102.3 %all-to-all-start = ((bf16[128,4,1536]{0,2,1:T(8,128)(2,1)}), bf16[128,4,1536]{0,2,1:T(8,128)(2,1)S(1)}, u32[]{:S(2)}, u32[]{:S(2)}) async-start(bf16[128,4,1536]{0,2,1:T(8,128)(2,1)} %bitcast), calls=%async_computation.1 | async-start | bytes 3145728 | tf_op jit(solution)/shard_map/all_to_all | solution.py:33
  690.6 135.2 %reduce-scatter.2.cloned.1.call-start = ((), (), s32[]{:S(2)}) async-start(), calls=%async_computation.5 | async-start | bytes 1769472 | tf_op jit(solution)/shard_map/reduce_scatter | solution.py:37
Sparse Core Ops, SparseCore 0:
  10.5 26.3 all-gather.3
  38.5 631.9 all-gather.5
  687.1 91.7 all-gather.7
  789.4 36.3 reduce-scatter.1
where the time goes:
time: 835 us; the launch traced here: 832 us
  waiting for transfers between devices  763 us (91%)
  matrix products  36.5 us (4%)
  local copies, waits for them, and re-layouts  15.1 us (2%)
  between operations  13.8 us (2%)
    all_gather x1, waiting for transfers between devices, local(): lax.all_gather(weight, 'row', axis=0, tiled=True)  634 us
    all_gather x1, waiting for transfers between devices, local(): all_hidden = lax.all_gather(hidden_grad, 'row', axis=0, tiled=True)  88.3 us
    all_gather x1, waiting for transfers between devices, local(): row_block = lax.all_gather(tokens, 'col', axis=1, tiled=True)  27.1 us
  transfers between devices with their start and end apart: 5, of which 4 were waited for; matrix products, arithmetic and copies ran while one was open for 4% of the time, Pallas kernels for 0%

commit v1 on v0

--- a/solution.py
+++ b/solution.py
@@ -22,15 +22,14 @@
 
 def local(tokens, weight, act_grad):
     row_block = lax.all_gather(tokens, "col", axis=1, tiled=True)
-    hidden_pre = jnp.dot(
-        row_block,
-        lax.all_gather(weight, "row", axis=0, tiled=True),
-        preferred_element_type=jnp.float32,
-    )
+    token_cols = lax.all_to_all(row_block, "row", split_axis=1, concat_axis=0, tiled=True)
+    partial_pre = jnp.dot(token_cols, weight, preferred_element_type=jnp.float32)
+    hidden_pre = lax.psum_scatter(
+        partial_pre.astype(jnp.bfloat16), "row", scatter_dimension=0, tiled=True
+    ).astype(jnp.float32)
     activation = gelu_tanh(hidden_pre).astype(jnp.bfloat16)
     hidden_grad = (act_grad.astype(jnp.float32) * gelu_slope(hidden_pre)).astype(jnp.bfloat16)
     all_hidden = lax.all_gather(hidden_grad, "row", axis=0, tiled=True)
-    token_cols = lax.all_to_all(row_block, "row", split_axis=1, concat_axis=0, tiled=True)
     weight_grad = lax.dot_general(
         token_cols, all_hidden, (((0,), (0,)), ((), ())), preferred_element_type=jnp.float32
     ).astype(jnp.bfloat16)

time: 835 us -> 272 us (0.33)
  waiting for transfers between devices: 763 us -> 166 us
  blocking collectives: 0 us -> 40.9 us
    all_gather x1 -> x0, waiting for transfers between devices: 634 us -> none  [local(): lax.all_gather(weight, 'row', axis=0, tiled=True)]
    reduce_scatter x0 -> x1, waiting for transfers between devices: none -> 59.9 us  [local(): lax.psum_scatter(partial_pre.astype(jnp.bfloat16), 'row', scatter_dimensi...]
    all_to_all x0 -> x1, blocking collectives: none -> 40.9 us  [local(): lax.all_to_all(row_block, 'row', split_axis=1, concat_axis=0, tiled=True)]
    all_gather x1, waiting for transfers between devices: 88.3 us -> 63.8 us  [local(): all_hidden = lax.all_gather(hidden_grad, 'row', axis=0, tiled=True)]
  transfers between devices with their start and end apart: 5 -> 4, of which waited for: 4 -> 4; matrix products, arithmetic and copies ran while one was open for 4% -> 8% of each run, Pallas kernels for 0% -> 0%
where the time goes in v1:
time: 272 us; the launch traced here: 269 us
  waiting for transfers between devices  166 us (61%)
  blocking collectives  40.9 us (15%)
  matrix products  29.9 us (11%)
  local copies, waits for them, and re-layouts  15.1 us (6%)
  between operations  13.8 us (5%)
  other arithmetic  3.44 us (1%)
    all_gather x1, waiting for transfers between devices, local(): all_hidden = lax.all_gather(hidden_grad, 'row', axis=0, tiled=True)  63.8 us
    reduce_scatter x1, waiting for transfers between devices, local(): lax.psum_scatter(partial_pre.astype(jnp.bfloat16), 'row', scatter_dimensi...  59.9 us
    all_to_all x1, blocking collectives, local(): lax.all_to_all(row_block, 'row', split_axis=1, concat_axis=0, tiled=True)  40.9 us
    all_gather x1, waiting for transfers between devices, local(): row_block = lax.all_gather(tokens, 'col', axis=1, tiled=True)  27.9 us
    unnamed x4, local copies, waits for them, and re-layouts  14.4 us
    reduce_scatter x1, waiting for transfers between devices, local(): lax.psum_scatter(lax.dot_general(all_hidden, weight, (((1,), (1,)), ((),...  14.2 us
    dot_general x1, matrix products, local(): lax.dot_general(all_hidden, weight, (((1,), (1,)), ((), ())), preferred_e...  10.3 us
    dot_general x1, matrix products, local(): jnp.dot(token_cols, weight, preferred_element_type=jnp.float32)  10.1 us
  transfers between devices with their start and end apart: 4, of which 4 were waited for; matrix products, arithmetic and copies ran while one was open for 8% of the time, Pallas kernels for 0%

profile of v1, /device:TPU:7, one launch (start us, length us, event | category | flops | bytes accessed | tf_op | source)
XLA Modules:
  0.0 269.1 jit_solution(439925751047804281)
XLA Ops:
  7.2 0.0 all-gather.3.cloned.1.call-start
  7.2 1.7 copy.8
  9.0 0.0 all-gather.3.cloned.1.call-update
  9.0 0.0 reduce-scatter.3.cloned.1.call-start
  9.0 27.9 %all-gather.3.cloned.1.call-done = bf16[128,6144]{0,1:T(8,128)(2,1)} async-done(((bf16[128,768]{0,1:T(8,128)(2,1)}), bf16[128,6144]{0,1:T(8,128)(2,1)}) %all-gather.3.cloned.1.call-update) | async-done | bytes 1572880 | tf_op jit(solution)/shard_map/all_gather | solution.py:24
  36.9 40.9 %all_to_all.19 = bf16[128,4,1536]{0,2,1:T(8,128)(2,1)S(1)} all-to-all(bf16[128,4,1536]{0,2,1:T(8,128)(2,1)} %bitcast.14), channel_id=1, replica_groups=mesh['row'=4,'col'=8] {'row'}, dimensions={1} | all-to-all | bytes 3145728 | tf_op jit(solution)/shard_map/all_to_all | solution.py:25
  77.8 0.7 copy.9
  78.5 10.1 %convolution_convert_fusion.1 = bf16[512,3072]{1,0:T(8,128)(2,1)} fusion(bf16[512,1536]{1,0:T(8,128)(2,1)S(1)} %bitcast.12, bf16[1536,3072]{1,0:T(8,128)(2,1)} %param.4), kind=kOutput, calls=%fused_computation.2 | convolution fusion | flops 4833411072 | bytes 14155776 | tf_op jit(solution)/shard_map/dot_general | solution.py:26
  88.5 0.0 copy-start
  88.5 0.0 reduce-scatter.3.cloned.1.call-update
  88.5 0.0 all-gather.5.cloned.1.call-start
  88.6 59.9 %reduce-scatter.3.cloned.1.call-done = bf16[128,3072]{1,0:T(8,128)(2,1)} async-done(((bf16[512,3072]{1,0:T(8,128)(2,1)}), bf16[128,3072]{1,0:T(8,128)(2,1)}) %reduce-scatter.3.cloned.1.call-update) | async-done | bytes 786448 | tf_op jit(solution)/shard_map/reduce_scatter | solution.py:27
  148.5 0.0 copy-done
  148.5 3.4 %fusion.8 = (bf16[128,3072]{1,0:T(8,128)(2,1)}, bf16[128,3072]{1,0:T(8,128)(2,1)}) fusion(bf16[128,3072]{1,0:T(8,128)(2,1)} %reduce-scatter.3.cloned.1.call-done, bf16[128,3072]{1,0:T(8,128)(2,1)S(1)} %copy-done), kind=kLoop, calls=%fused_computation.18 | loop fusion | flops 9043968 | bytes 3145728 | tf_op jit(solution)/shard_map/convert_element_type | solution.py:31
  152.0 0.0 all-gather.5.cloned.1.call-update
  152.0 0.0 reduce-scatter.5.cloned.1.call-start
  152.1 63.8 %all-gather.5.cloned.1.call-done = bf16[512,3072]{1,0:T(8,128)(2,1)} async-done(((bf16[128,3072]{1,0:T(8,128)(2,1)}), bf16[512,3072]{1,0:T(8,128)(2,1)}) %all-gather.5.cloned.1.call-update) | async-done | bytes 3145744 | tf_op jit(solution)/shard_map/all_gather | solution.py:32
  215.8 10.3 %convolution_convert_fusion.2 = bf16[512,1536]{1,0:T(8,128)(2,1)} fusion(bf16[512,3072]{1,0:T(8,128)(2,1)} %all-gather.5.cloned.1.call-done, bf16[1536,3072]{1,0:T(8,128)(2,1)} %param.4), kind=kOutput, calls=%fused_computation.10 | convolution fusion | flops 4832624640 | bytes 14155776 | tf_op jit(solution)/shard_map/dot_general | solution.py:37
  226.2 0.0 reduce-scatter.5.cloned.1.call-update
  226.2 9.5 %fusion = bf16[1536,3072]{0,1:T(8,128)(2,1)} fusion(bf16[512,3072]{1,0:T(8,128)(2,1)} %all-gather.5.cloned.1.call-done, bf16[512,1536]{1,0:T(8,128)(2,1)S(1)} %bitcast.13), kind=kOutput, calls=%fused_computation.1 | convolution fusion | flops 4836556800 | bytes 14155776 | tf_op jit(solution)/shard_map/dot_general | solution.py:33
  235.7 12.7 %copy.10 = bf16[1536,3072]{1,0:T(8,128)(2,1)} copy(bf16[1536,3072]{0,1:T(8,128)(2,1)} %fusion) | data formatting | bytes 18874368
  248.4 14.2 %reduce-scatter.5.cloned.1.call-done = bf16[64,1536]{1,0:T(8,128)(2,1)} async-done(((bf16[512,1536]{1,0:T(8,128)(2,1)}), bf16[64,1536]{1,0:T(8,128)(2,1)}) %reduce-scatter.5.cloned.1.call-update) | async-done | bytes 196624 | tf_op jit(solution)/shard_map/reduce_scatter | solution.py:36
Async XLA Ops:
  7.2 29.7 %all-gather.3.cloned.1.call-start = ((), (), s32[]{:S(2)}) async-start(), calls=%async_computation.3 | async-start | bytes 1769472 | tf_op jit(solution)/shard_map/all_gather | solution.py:24
  9.0 139.6 %reduce-scatter.3.cloned.1.call-start = ((), (), s32[]{:S(2)}) async-start(), calls=%async_computation.4 | async-start | bytes 3932160 | tf_op jit(solution)/shard_map/reduce_scatter | solution.py:27
  88.5 60.0 %copy-start = (bf16[128,3072]{1,0:T(8,128)(2,1)S(1)}, bf16[128,3072]{1,0:T(8,128)(2,1)}, u32[]{:S(2)}) copy-start(bf16[128,3072]{1,0:T(8,128)(2,1)} %param.5) | copy-start | bytes 2359300
  88.5 127.3 %all-gather.5.cloned.1.call-start = ((), (), s32[]{:S(2)}) async-start(), calls=%async_computation.5 | async-start | bytes 3932160 | tf_op jit(solution)/shard_map/all_gather | solution.py:32
  152.0 110.5 %reduce-scatter.5.cloned.1.call-start = ((), (), s32[]{:S(2)}) async-start(), calls=%async_computation.6 | async-start | bytes 1769472 | tf_op jit(solution)/shard_map/reduce_scatter | solution.py:36
Sparse Core Ops, SparseCore 0:
  10.5 26.3 all-gather.2
  88.7 59.8 reduce-scatter.2
  152.1 63.6 all-gather.4
  226.3 36.2 reduce-scatter.4

commit v2 on v1

v2 whole, which is shorter than its diff:
```python
import functools

import jax
import jax.numpy as jnp
from jax import lax
from jax.experimental import pallas as pl
from jax.experimental.pallas import tpu as pltpu
from jax.sharding import PartitionSpec as P

root_two_pi = 0.7978845608028654
cubic_coef = 0.044715
LAG = 1
WIDTH = 256


def grid_kernel(
    n, count, width, rows, lag,
    x_ref, xt_ref, w_hbm, g_ref,
    act_ref, dx_ref, dw_hbm,
    w_v, p_v, stage, from_low, from_high, hidden, dx_acc, dw_v,
    w_sem, dw_sem, low_sem, high_sem, ag_sem, rs_send, up_send, down_send,
):
    z = lax.axis_index("row")
    bf16, f32 = jnp.bfloat16, jnp.float32

    def w_copy(k):
        cols = pl.ds(pl.multiple_of(k * width, width), width)
        return pltpu.make_async_copy(w_hbm.at[:, cols], w_v.at[k], w_sem.at[k])

    def dw_copy(k):
        cols = pl.ds(pl.multiple_of(k * width, width), width)
        return pltpu.make_async_copy(dw_v.at[lax.rem(k, 2)], dw_hbm.at[:, cols], dw_sem.at[lax.rem(k, 2)])

    def block(t):
        return pl.ds(t * rows, rows)

    def send_up(src, dst, send, recv):
        return pltpu.make_async_remote_copy(src, dst, send, recv, device_id={"row": z + 1}, device_id_type=pl.DeviceIdType.MESH)

    def send_down(src, dst, send, recv):
        return pltpu.make_async_remote_copy(src, dst, send, recv, device_id={"row": z - 1}, device_id_type=pl.DeviceIdType.MESH)

    def rs_up(k, t):
        return send_up(stage.at[k, block(t)], from_low.at[k, block(t)], rs_send.at[k, t], low_sem.at[k, t])

    def rs_down(k, t):
        return send_down(stage.at[k, block(t)], from_high.at[k, block(t)], rs_send.at[k, t], high_sem.at[k, t])

    def ag_up(k, t):
        return send_up(hidden.at[k, block(t)], hidden.at[k, block(t)], up_send.at[k, t], ag_sem.at[k, t])

    def ag_down(k, t):
        return send_down(hidden.at[k, block(t)], hidden.at[k, block(t)], down_send.at[k, t], ag_sem.at[k, t])

    def inside(k):
        return jnp.logical_and(k >= 0, k < count)

    def both(a, b):
        return jnp.logical_and(a, b)

    def first_matmul(k):
        w_copy(k).wait()
        p_v[k] = jnp.dot(x_ref[...], w_v[k], preferred_element_type=f32)

    def start_w(k, carry):
        w_copy(k).start()
        return carry

    lax.fori_loop(0, count, start_w, 0)

    barrier = pltpu.get_barrier_semaphore()

    @pl.when(z > 0)
    def _():
        pl.semaphore_signal(barrier, inc=1, device_id={"row": z - 1}, device_id_type=pl.DeviceIdType.MESH)

    @pl.when(z < n - 1)
    def _():
        pl.semaphore_signal(barrier, inc=1, device_id={"row": z + 1}, device_id_type=pl.DeviceIdType.MESH)

    @pl.when(both(z > 0, z < n - 1))
    def _():
        pl.semaphore_wait(barrier, 2)

    @pl.when(jnp.logical_or(z == 0, z == n - 1))
    def _():
        pl.semaphore_wait(barrier, 1)

    dx_acc[...] = jnp.zeros_like(dx_acc)
    first_matmul(0)

    def step(s, carry):
        up_k = s - lag * z
        for t in range(n - 1, 0, -1):

            @pl.when(both(t > z, inside(up_k)))
            def _():
                @pl.when(z > 0)
                def _():
                    rs_up(up_k, t).wait_recv()
                    stage[up_k, block(t)] = (
                        p_v[up_k, block(t)] + from_low[up_k, block(t)].astype(f32)
                    ).astype(bf16)

                @pl.when(z == 0)
                def _():
                    stage[up_k, block(t)] = p_v[up_k, block(t)].astype(bf16)

                rs_up(up_k, t).start()

        down_k = s - lag * (n - 1 - z)
        for t in range(n - 1):

            @pl.when(both(t < z, inside(down_k)))
            def _():
                @pl.when(z < n - 1)
                def _():
                    rs_down(down_k, t).wait_recv()
                    stage[down_k, block(t)] = (
                        p_v[down_k, block(t)] + from_high[down_k, block(t)].astype(f32)
                    ).astype(bf16)

                @pl.when(z == n - 1)
                def _():
                    stage[down_k, block(t)] = p_v[down_k, block(t)].astype(bf16)

                rs_down(down_k, t).start()

        own_k = s - lag * (n - 1)

        @pl.when(inside(own_k))
        def _():
            mine = pl.ds(pl.multiple_of(z * rows, rows), rows)
            cols = pl.ds(pl.multiple_of(own_k * width, width), width)

            @pl.when(z > 0)
            def _():
                rs_up(own_k, z).wait_recv()
                p_v[own_k, mine] += from_low[own_k, mine].astype(f32)

            @pl.when(z < n - 1)
            def _():
                rs_down(own_k, z).wait_recv()
                p_v[own_k, mine] += from_high[own_k, mine].astype(f32)

            u = p_v[own_k, mine]
            angle = jnp.tanh(root_two_pi * (u + cubic_coef * u * u * u))
            act_ref[:, cols] = (0.5 * u * (1.0 + angle)).astype(bf16)
            slope = 0.5 * (1.0 + angle) + 0.5 * u * (1.0 - angle * angle) * root_two_pi * (
                1.0 + 3.0 * cubic_coef * u * u
            )
            hidden[own_k, mine] = (g_ref[:, cols].astype(f32) * slope).astype(bf16)

            @pl.when(z < n - 1)
            def _():
                ag_up(own_k, z).start()

            @pl.when(z > 0)
            def _():
                ag_down(own_k, z).start()

        for t in range(n):
            low_k = s - lag * (n - 1) - lag * (z - t)

            @pl.when(both(t < z, inside(low_k)))
            def _():
                ag_up(low_k, t).wait_recv()

                @pl.when(z < n - 1)
                def _():
                    ag_up(low_k, t).start()

            high_k = s - lag * (n - 1) - lag * (t - z)

            @pl.when(both(t > z, inside(high_k)))
            def _():
                ag_down(high_k, t).wait_recv()

                @pl.when(z > 0)
                def _():
                    ag_down(high_k, t).start()

        @pl.when(s + 1 < count)
        def _():
            first_matmul(s + 1)

        last_k = s - 2 * lag * (n - 1)

        @pl.when(inside(last_k))
        def _():
            @pl.when(last_k >= 2)
            def _():
                dw_copy(last_k - 2).wait()

            dw_v[lax.rem(last_k, 2)] = jnp.dot(
                xt_ref[...], hidden[last_k], preferred_element_type=f32
            ).astype(bf16)
            dw_copy(last_k).start()
            dx_acc[...] += lax.dot_general(
                hidden[last_k], w_v[last_k], (((1,), (1,)), ((), ())), preferred_element_type=f32
            )

        return carry

    lax.fori_loop(0, count + 2 * lag * (n - 1), step, 0)
    dx_ref[...] = dx_acc[...].astype(bf16)

    def finish(k, carry):
        for t in range(n):

            @pl.when(t > z)
            def _():
                rs_up(k, t).wait_send()

            @pl.when(t < z)
            def _():
                rs_down(k, t).wait_send()

            @pl.when(both(t <= z, z < n - 1))
            def _():
                ag_up(k, t).wait_send()

            @pl.when(both(t >= z, z > 0))
            def _():
                ag_down(k, t).wait_send()

        return carry

    lax.fori_loop(0, count, finish, 0)
    for k in range(max(0, count - 2), count):
        dw_copy(k).wait()


def pick_width(units):
    width = min(WIDTH, units)
    while units % width:
        width -= 128
    return width


def grid_call(n, x, weight, act_grad):
    tokens, depth = x.shape
    rows, units = act_grad.shape
    width = pick_width(units)
    count = units // width
    bf16, f32 = jnp.bfloat16, jnp.float32
    vmem = pl.BlockSpec(memory_space=pltpu.VMEM)
    hbm = pl.BlockSpec(memory_space=pl.ANY)
    chunks = (count, tokens, width)
    dma = pltpu.SemaphoreType.DMA
    return pl.pallas_call(
        functools.partial(grid_kernel, n, count, width, rows, LAG),
        out_shape=(
            jax.ShapeDtypeStruct((rows, units), bf16),
            jax.ShapeDtypeStruct((tokens, depth), bf16),
            jax.ShapeDtypeStruct((depth, units), bf16),
        ),
        in_specs=[vmem, vmem, hbm, vmem],
        out_specs=(vmem, vmem, hbm),
        scratch_shapes=[
            pltpu.VMEM((count, depth, width), bf16),
            pltpu.VMEM(chunks, f32),
            pltpu.VMEM(chunks, bf16),
            pltpu.VMEM(chunks, bf16),
            pltpu.VMEM(chunks, bf16),
            pltpu.VMEM(chunks, bf16),
            pltpu.VMEM((tokens, depth), f32),
            pltpu.VMEM((2, depth, width), bf16),
            dma((count,)),
            dma((2,)),
            dma((count, n)),
            dma((count, n)),
            dma((count, n)),
            dma((count, n)),
            dma((count, n)),
            dma((count, n)),
        ],
        compiler_params=pltpu.CompilerParams(
            collective_id=0, has_side_effects=True, vmem_limit_bytes=60 * 1024 * 1024
        ),
        cost_estimate=pl.CostEstimate(
            flops=6 * tokens * depth * units, bytes_accessed=4 * depth * units, transcendentals=rows * units
        ),
    )(x, x.T, weight, act_grad)


def local(n, tokens, weight, act_grad):
    row_block = lax.all_gather(tokens, "col", axis=1, tiled=True)
    token_cols = lax.all_to_all(row_block, "row", split_axis=1, concat_axis=0, tiled=True)
    activation, partial_grad, weight_grad = grid_call(n, token_cols, weight, act_grad)
    input_grad = lax.psum_scatter(partial_grad, "col", scatter_dimension=0, tiled=True)
    return (activation, input_grad, weight_grad)


def solution(mesh):
    placed = (P("row", "col"), P("row", "col"), P("row", "col"))
    return jax.shard_map(
        functools.partial(local, mesh.shape["row"]),
        mesh=mesh,
        in_specs=placed,
        out_specs=(P("row", "col"), P("col", "row"), P("row", "col")),
        check_vma=False,
    )
```

time: 272 us -> 231 us (0.85)
  waiting for transfers between devices: 166 us -> 68 us
  Pallas kernels: 0 us -> 91.4 us
  matrix products: 29.9 us -> 0 us
  other arithmetic: 3.44 us -> 0 us
    pallas_call x0 -> x1, Pallas kernels: none -> 91.4 us  [grid_call(): pl.pallas_call(functools.partial(grid_kernel, n, count, width, rows, LAG)...]
    all_gather x1 -> x0, waiting for transfers between devices: 63.8 us -> none  [local(): all_hidden = lax.all_gather(hidden_grad, 'row', axis=0, tiled=True)]
    reduce_scatter x2 -> x1, waiting for transfers between devices: 74.1 us -> 38.9 us  [local(): lax.psum_scatter(partial_grad, 'col', scatter_dimension=0, tiled=True)]
    dot_general x3 -> x0, matrix products: 29.9 us -> none  [the longest x1 10.3 us: local(): lax.dot_general(all_hidden, weight, (((1,), (1,)), ((), ())), preferred_e...]
    unnamed x4, local copies, waits for them, and re-layouts: 14.4 us -> 9.15 us
    convert_element_type x1 -> x0, other arithmetic: 3.44 us -> none  [local(): (act_grad.astype(jnp.float32) * gelu_slope(hidden_pre)).astype(jnp.bfloat16)]
  transfers between devices with their start and end apart: 4 -> 2, of which waited for: 4 -> 2; matrix products, arithmetic and copies ran while one was open for 8% -> 0% of each run, Pallas kernels for 0% -> 0%
where the time goes in v2:
time: 231 us; the launch traced here: 228 us
  Pallas kernels  91.4 us (40%)
  waiting for transfers between devices  68 us (29%)
  blocking collectives  40.7 us (18%)
  between operations  14.1 us (6%)
  local copies, waits for them, and re-layouts  14 us (6%)
    pallas_call x1, Pallas kernels, grid_call(): pl.pallas_call(functools.partial(grid_kernel, n, count, width, rows, LAG)...  91.4 us
    all_to_all x1, blocking collectives, local(): lax.all_to_all(row_block, 'row', split_axis=1, concat_axis=0, tiled=True)  40.7 us
    reduce_scatter x1, waiting for transfers between devices, local(): lax.psum_scatter(partial_grad, 'col', scatter_dimension=0, tiled=True)  38.9 us
    all_gather x1, waiting for transfers between devices, local(): row_block = lax.all_gather(tokens, 'col', axis=1, tiled=True)  28.4 us
    unnamed x4, local copies, waits for them, and re-layouts  9.15 us
  transfers between devices with their start and end apart: 2, of which 2 were waited for; matrix products, arithmetic and copies ran while one was open for 0% of the time, Pallas kernels for 0%

profile of v2, /device:TPU:7, one launch (start us, length us, event | category | flops | bytes accessed | tf_op | source)
XLA Modules:
  0.0 228.3 jit_solution(7053717678810391953)
XLA Ops:
  7.2 0.0 all-gather.2.cloned.1.call-start
  7.2 0.7 all-gather.2.cloned.1.call-update
  7.9 0.0 reduce-scatter.2.cloned.1.call-start
  7.9 28.4 %all-gather.2.cloned.1.call-done = bf16[128,6144]{1,0:T(8,128)(2,1)} async-done(((bf16[128,768]{1,0:T(8,128)(2,1)}), bf16[128,6144]{1,0:T(8,128)(2,1)}) %all-gather.2.cloned.1.call-update) | async-done | bytes 1572880 | tf_op jit(solution)/shard_map/all_gather | solution.py:288
  36.3 1.9 copy.8
  38.2 40.7 %all_to_all.19 = bf16[128,4,1536]{0,2,1:T(8,128)(2,1)S(1)} all-to-all(bf16[128,4,1536]{0,2,1:T(8,128)(2,1)S(1)} %bitcast.11), channel_id=1, replica_groups=mesh['row'=4,'col'=8] {'row'}, dimensions={1} | all-to-all | bytes 3145728 | tf_op jit(solution)/shard_map/all_to_all | solution.py:289
  78.9 1.4 fusion
  80.3 1.6 copy.10.x_ref
  81.9 91.4 %shard_map.58 = (bf16[128,3072]{1,0:T(8,128)(2,1)}, bf16[512,1536]{1,0:T(8,128)(2,1)}, bf16[1536,3072]{1,0:T(8,128)(2,1)}) custom-call(bf16[512,1536]{1,0:T(8,128)(2,1)} %copy.10.x_ref, bf16[1536,512]{1,0:T(8,128)(2,1)} %get-tuple-element.9.xt_ref, bf16[1536,3072]{1,0:T(8,128)(2,1)} %w_hbm.1, bf16[128,3072]{1,0:T(8,128)(2,1)} %g_ref.1), custom_call_target="tpu_custom_call" | custom-call | flops 14495514624 | bytes 18874368 | tf_op jit(solution)/shard_map/pallas_call | solution.py:251
  173.3 0.0 copy-start
  173.3 0.0 reduce-scatter.2.cloned.1.call-update
  173.3 38.9 %reduce-scatter.2.cloned.1.call-done = bf16[64,1536]{1,0:T(8,128)(2,1)} async-done(((bf16[512,1536]{1,0:T(8,128)(2,1)}), bf16[64,1536]{1,0:T(8,128)(2,1)}) %reduce-scatter.2.cloned.1.call-update) | async-done | bytes 196624 | tf_op jit(solution)/shard_map/reduce_scatter | solution.py:291
  212.3 0.0 copy-done
  212.3 0.9 copy.17
  213.1 8.3 %copy.18 = bf16[1536,3072]{1,0:T(8,128)(2,1)} copy(bf16[1536,3072]{1,0:T(8,128)(2,1)} %get-tuple-element.16) | data formatting | bytes 18874368
Async XLA Ops:
  7.2 29.2 %all-gather.2.cloned.1.call-start = ((), (), s32[]{:S(2)}) async-start(), calls=%async_computation.2 | async-start | bytes 1769472 | tf_op jit(solution)/shard_map/all_gather | solution.py:288
  7.9 204.4 %reduce-scatter.2.cloned.1.call-start = ((), (), s32[]{:S(2)}) async-start(), calls=%async_computation.3 | async-start | bytes 1769472 | tf_op jit(solution)/shard_map/reduce_scatter | solution.py:291
  173.3 39.0 %copy-start = (bf16[128,3072]{1,0:T(8,128)(2,1)S(1)}, bf16[128,3072]{1,0:T(8,128)(2,1)}, u32[]{:S(2)}) copy-start(bf16[128,3072]{1,0:T(8,128)(2,1)} %get-tuple-element.14) | copy-start | bytes 2359300
Sparse Core Ops, SparseCore 0:
  9.9 26.3 all-gather.1
  173.5 38.7 reduce-scatter.1

commit v3 on v2

--- a/solution.py
+++ b/solution.py
@@ -11,17 +11,32 @@
 cubic_coef = 0.044715
 LAG = 1
 WIDTH = 256
+CHIPS = 4
+CORES = 2
 
 
 def grid_kernel(
-    n, count, width, rows, lag,
-    x_ref, xt_ref, w_hbm, g_ref,
+    n, count, width, rows, lag, plane,
+    x_in, w_hbm, g_ref,
     act_ref, dx_ref, dw_hbm,
-    w_v, p_v, stage, from_low, from_high, hidden, dx_acc, dw_v,
+    w_v, p_v, stage, from_low, from_high, hidden, dx_acc, dw_v, xt_ref,
     w_sem, dw_sem, low_sem, high_sem, ag_sem, rs_send, up_send, down_send,
+    *extra,
 ):
     z = lax.axis_index("row")
     bf16, f32 = jnp.bfloat16, jnp.float32
+    if plane:
+        (
+            x_ref, token_parts, z_parts, pair_out, pair_in, chip_out, chip_in,
+            spread_send, spread_recv, z_send, z_recv, chip_send, chip_recv, pair_send, pair_recv,
+            sum_pair_send, sum_pair_recv, sum_chip_send, sum_chip_recv,
+        ) = extra
+        col = lax.axis_index("col")
+        chip, core = col // CORES, col % CORES
+        half = x_in.shape[1]
+        part = rows // CHIPS
+    else:
+        x_ref = x_in
 
     def w_copy(k):
         cols = pl.ds(pl.multiple_of(k * width, width), width)
@@ -68,23 +83,150 @@
 
     lax.fori_loop(0, count, start_w, 0)
 
-    barrier = pltpu.get_barrier_semaphore()
-
-    @pl.when(z > 0)
-    def _():
-        pl.semaphore_signal(barrier, inc=1, device_id={"row": z - 1}, device_id_type=pl.DeviceIdType.MESH)
-
-    @pl.when(z < n - 1)
-    def _():
-        pl.semaphore_signal(barrier, inc=1, device_id={"row": z + 1}, device_id_type=pl.DeviceIdType.MESH)
-
-    @pl.when(both(z > 0, z < n - 1))
-    def _():
-        pl.semaphore_wait(barrier, 2)
-
-    @pl.when(jnp.logical_or(z == 0, z == n - 1))
-    def _():
-        pl.semaphore_wait(barrier, 1)
+    def line_barrier():
+        barrier = pltpu.get_barrier_semaphore()
+
+        @pl.when(z > 0)
+        def _():
+            pl.semaphore_signal(barrier, inc=1, device_id={"row": z - 1}, device_id_type=pl.DeviceIdType.MESH)
+
+        @pl.when(z < n - 1)
+        def _():
+            pl.semaphore_signal(barrier, inc=1, device_id={"row": z + 1}, device_id_type=pl.DeviceIdType.MESH)
+
+        @pl.when(both(z > 0, z < n - 1))
+        def _():
+            pl.semaphore_wait(barrier, 2)
+
+        @pl.when(jnp.logical_or(z == 0, z == n - 1))
+        def _():
+            pl.semaphore_wait(barrier, 1)
+
+    def to(row, column):
+        return {"device_id": {"row": row, "col": column}, "device_id_type": pl.DeviceIdType.MESH}
+
+    def other_chip(d):
+        return ((chip + d) % CHIPS) * CORES + core
+
+    def pair():
+        return chip * CORES + 1 - core
+
+    def spread(d):
+        target = (chip + d) % CHIPS
+        return pltpu.make_async_remote_copy(
+            x_in.at[pl.ds(pl.multiple_of(target * part, part), part)], token_parts.at[chip],
+            spread_send.at[d], spread_recv.at[d], **to(z, other_chip(d)),
+        )
+
+    def across(d):
+        target = (z + d) % n
+        return pltpu.make_async_remote_copy(
+            token_parts.at[target], z_parts.at[z], z_send.at[d], z_recv.at[d], **to(target, col)
+        )
+
+    def place(origin, source_chip, source_core):
+        return (
+            pl.ds(pl.multiple_of(origin * rows + source_chip * part, part), part),
+            pl.ds(pl.multiple_of(source_core * half, half), half),
+        )
+
+    def share(dz, d):
+        origin = (z - dz + n) % n
+        return pltpu.make_async_remote_copy(
+            z_parts.at[origin], x_ref.at[place(origin, chip, core)],
+            chip_send.at[dz, d], chip_recv.at[dz, d], **to(z, other_chip(d)),
+        )
+
+    def to_pair(dz, d):
+        origin = (z - dz + n) % n
+        where = place(origin, (chip - d + CHIPS) % CHIPS, core)
+        return pltpu.make_async_remote_copy(
+            x_ref.at[where], x_ref.at[where], pair_send.at[dz, d], pair_recv.at[dz, d], **to(z, pair())
+        )
+
+    def gather_tokens():
+        for d in range(1, CHIPS):
+            spread(d).start()
+        token_parts[chip] = x_in[pl.ds(pl.multiple_of(chip * part, part), part), :]
+        for d in range(1, CHIPS):
+            spread(d).wait_recv()
+        for d in range(1, n):
+            across(d).start()
+        z_parts[z] = token_parts[z]
+        for dz in range(n):
+            origin = (z - dz + n) % n
+            if dz:
+                across(dz).wait_recv()
+            for d in (2, 1, 3):
+                share(dz, d).start()
+            x_ref[place(origin, chip, core)] = z_parts[origin]
+            to_pair(dz, 0).start()
+        for dz in range(n):
+            for d in (1, 3, 2):
+                share(dz, d).wait_recv()
+                to_pair(dz, d).start()
+        for dz in range(n):
+            for d in range(CHIPS):
+                to_pair(dz, d).wait_recv()
+
+    def end_gather():
+        for d in range(1, CHIPS):
+            spread(d).wait_send()
+        for d in range(1, n):
+            across(d).wait_send()
+        for dz in range(n):
+            for d in range(CHIPS):
+                to_pair(dz, d).wait_send()
+                if d:
+                    share(dz, d).wait_send()
+
+    def sum_rows(d, which):
+        size = dx_ref.shape[0]
+        return pl.ds(pl.multiple_of((((chip + d) % CHIPS) * CORES + which) * size, size), size)
+
+    def sum_pair(d):
+        return pltpu.make_async_remote_copy(
+            pair_out.at[d], pair_in.at[d], sum_pair_send.at[d], sum_pair_recv.at[d], **to(z, pair())
+        )
+
+    def sum_chip(d):
+        return pltpu.make_async_remote_copy(
+            chip_out.at[d], chip_in.at[d], sum_chip_send.at[d], sum_chip_recv.at[d], **to(z, other_chip(d))
+        )
+
+    def scatter_sum():
+        order = (2, 1, 3, 0)
+        for d in order:
+            pair_out[d] = dx_acc[sum_rows(d, 1 - core), :].astype(bf16)
+            sum_pair(d).start()
+        for d in order:
+            sum_pair(d).wait_recv()
+            both_cores = dx_acc[sum_rows(d, core), :] + pair_in[d].astype(f32)
+            if d:
+                chip_out[d] = both_cores.astype(bf16)
+                sum_chip(d).start()
+            else:
+                total = both_cores
+        for d in range(1, CHIPS):
+            sum_chip(d).wait_recv()
+            total += chip_in[d].astype(f32)
+        dx_ref[...] = total.astype(bf16)
+        for d in order:
+            sum_pair(d).wait_send()
+            if d:
+                sum_chip(d).wait_send()
+
+    if plane:
+        barrier = pltpu.get_barrier_semaphore()
+        for d in range(1, n):
+            pl.semaphore_signal(barrier, inc=1, **to((z + d) % n, col))
+        for d in range(1, CHIPS):
+            pl.semaphore_signal(barrier, inc=1, **to(z, other_chip(d)))
+        pl.semaphore_signal(barrier, inc=1, **to(z, pair()))
+        pl.semaphore_wait(barrier, n - 1 + CHIPS)
+        gather_tokens()
+    else:
+        line_barrier()
 
     dx_acc[...] = jnp.zeros_like(dx_acc)
     first_matmul(0)
@@ -184,6 +326,10 @@
         def _():
             first_matmul(s + 1)
 
+        @pl.when(s == 1)
+        def _():
+            xt_ref[...] = x_ref[...].T
+
         last_k = s - 2 * lag * (n - 1)
 
         @pl.when(inside(last_k))
@@ -203,7 +349,11 @@
         return carry
 
     lax.fori_loop(0, count + 2 * lag * (n - 1), step, 0)
-    dx_ref[...] = dx_acc[...].astype(bf16)
+    if plane:
+        scatter_sum()
+        end_gather()
+    else:
+        dx_ref[...] = dx_acc[...].astype(bf16)
 
     def finish(k, carry):
         for t in range(n):
@@ -238,9 +388,10 @@
     return width
 
 
-def grid_call(n, x, weight, act_grad):
-    tokens, depth = x.shape
+def grid_call(n, plane, x, weight, act_grad):
     rows, units = act_grad.shape
+    depth = weight.shape[0]
+    tokens = n * rows
     width = pick_width(units)
     count = units // width
     bf16, f32 = jnp.bfloat16, jnp.float32
@@ -248,46 +399,55 @@
     hbm = pl.BlockSpec(memory_space=pl.ANY)
     chunks = (count, tokens, width)
     dma = pltpu.SemaphoreType.DMA
+    sum_rows = tokens // (CHIPS * CORES) if plane else tokens
+    scratch = [
+        pltpu.VMEM((count, depth, width), bf16),
+        pltpu.VMEM(chunks, f32),
+        pltpu.VMEM(chunks, bf16),
+        pltpu.VMEM(chunks, bf16),
+        pltpu.VMEM(chunks, bf16),
+        pltpu.VMEM(chunks, bf16),
+        pltpu.VMEM((tokens, depth), f32),
+        pltpu.VMEM((2, depth, width), bf16),
+        pltpu.VMEM((depth, tokens), bf16),
+        dma((count,)),
+        dma((2,)),
+    ] + [dma((count, n))] * 6
+    if plane:
+        part = (rows // CHIPS, x.shape[1])
+        scratch += [
+            pltpu.VMEM((tokens, depth), bf16),
+            pltpu.VMEM((CHIPS,) + part, bf16),
+            pltpu.VMEM((n,) + part, bf16),
+        ]
+        scratch += [pltpu.VMEM((CHIPS, sum_rows, depth), bf16)] * 4
+        scratch += [dma((CHIPS,))] * 2 + [dma((n,))] * 2 + [dma((n, CHIPS))] * 4 + [dma((CHIPS,))] * 4
     return pl.pallas_call(
-        functools.partial(grid_kernel, n, count, width, rows, LAG),
+        functools.partial(grid_kernel, n, count, width, rows, LAG, plane),
         out_shape=(
             jax.ShapeDtypeStruct((rows, units), bf16),
-            jax.ShapeDtypeStruct((tokens, depth), bf16),
+            jax.ShapeDtypeStruct((sum_rows, depth), bf16),
             jax.ShapeDtypeStruct((depth, units), bf16),
         ),
-        in_specs=[vmem, vmem, hbm, vmem],
+        in_specs=[vmem, hbm, vmem],
         out_specs=(vmem, vmem, hbm),
-        scratch_shapes=[
-            pltpu.VMEM((count, depth, width), bf16),
-            pltpu.VMEM(chunks, f32),
-            pltpu.VMEM(chunks, bf16),
-            pltpu.VMEM(chunks, bf16),
-            pltpu.VMEM(chunks, bf16),
-            pltpu.VMEM(chunks, bf16),
-            pltpu.VMEM((tokens, depth), f32),
-            pltpu.VMEM((2, depth, width), bf16),
-            dma((count,)),
-            dma((2,)),
-            dma((count, n)),
-            dma((count, n)),
-            dma((count, n)),
-            dma((count, n)),
-            dma((count, n)),
-            dma((count, n)),
-        ],
+        scratch_shapes=scratch,
         compiler_params=pltpu.CompilerParams(
             collective_id=0, has_side_effects=True, vmem_limit_bytes=60 * 1024 * 1024
         ),
         cost_estimate=pl.CostEstimate(
             flops=6 * tokens * depth * units, bytes_accessed=4 * depth * units, transcendentals=rows * units
         ),
-    )(x, x.T, weight, act_grad)
-
-
-def local(n, tokens, weight, act_grad):
+    )(x, weight, act_grad)
+
+
+def local(n, columns, tokens, weight, act_grad):
+    rows, part = tokens.shape
+    if n == CHIPS and columns == CHIPS * CORES and rows % (16 * CHIPS) == 0 and part % 128 == 0:
+        return grid_call(n, True, tokens, weight, act_grad)
     row_block = lax.all_gather(tokens, "col", axis=1, tiled=True)
     token_cols = lax.all_to_all(row_block, "row", split_axis=1, concat_axis=0, tiled=True)
-    activation, partial_grad, weight_grad = grid_call(n, token_cols, weight, act_grad)
+    activation, partial_grad, weight_grad = grid_call(n, False, token_cols, weight, act_grad)
     input_grad = lax.psum_scatter(partial_grad, "col", scatter_dimension=0, tiled=True)
     return (activation, input_grad, weight_grad)
 
@@ -295,7 +455,7 @@
 def solution(mesh):
     placed = (P("row", "col"), P("row", "col"), P("row", "col"))
     return jax.shard_map(
-        functools.partial(local, mesh.shape["row"]),
+        functools.partial(local, mesh.shape["row"], mesh.shape["col"]),
         mesh=mesh,
         in_specs=placed,
         out_specs=(P("row", "col"), P("col", "row"), P("row", "col")),

time: 231 us -> 137 us (0.59)
  the two profiles are of different devices: /device:TPU:7 before, /device:TPU:0 now
where the time goes in v3:
time: 137 us
  Pallas kernels  125 us (91%)
  local copies, waits for them, and re-layouts  11.9 us (9%)
    pallas_call x1, Pallas kernels, grid_call(): pl.pallas_call(functools.partial(grid_kernel, n, count, width, rows, LAG,...  125 us
    unnamed x3, local copies, waits for them, and re-layouts  11.9 us

profile of v3, /device:TPU:0, one launch (start us, length us, event | category | flops | bytes accessed | tf_op | source)
XLA Modules:
  0.0 137.2 jit_solution(1486475883343286711)
XLA Ops:
  0.6 124.6 %shard_map.58 = (bf16[128,3072]{1,0:T(8,128)(2,1)}, bf16[64,1536]{1,0:T(8,128)(2,1)}, bf16[1536,3072]{1,0:T(8,128)(2,1)}) custom-call(bf16[128,768]{1,0:T(8,128)(2,1)} %x_in.1, bf16[1536,3072]{1,0:T(8,128)(2,1)} %w_hbm.1, bf16[128,3072]{1,0:T(8,128)(2,1)} %g_ref.1), custom_call_target="tpu_custom_call" | custom-call | flops 14495514624 | bytes 18874368 | tf_op jit(solution)/shard_map/pallas_call | solution.py:425
  125.2 2.1 %copy.9 = bf16[128,3072]{1,0:T(8,128)(2,1)} copy(bf16[128,3072]{1,0:T(8,128)(2,1)} %get-tuple-element.6) | data formatting | bytes 1572864
  127.3 1.6 %copy.10 = bf16[64,1536]{1,0:T(8,128)(2,1)} copy(bf16[64,1536]{1,0:T(8,128)(2,1)} %get-tuple-element.7) | data formatting | bytes 393216
  128.9 8.3 %copy.11 = bf16[1536,3072]{1,0:T(8,128)(2,1)} copy(bf16[1536,3072]{1,0:T(8,128)(2,1)} %get-tuple-element.8) | data formatting | bytes 18874368

commit v4 on v3

--- a/solution.py
+++ b/solution.py
@@ -17,10 +17,10 @@
 
 def grid_kernel(
     n, count, width, rows, lag, plane,
-    x_in, w_hbm, g_ref,
+    x_in, w_hbm, g_hbm,
     act_ref, dx_ref, dw_hbm,
     w_v, p_v, stage, from_low, from_high, hidden, dx_acc, dw_v, xt_ref,
-    w_sem, dw_sem, low_sem, high_sem, ag_sem, rs_send, up_send, down_send,
+    g_ref, g_sem, w_sem, dw_sem, low_sem, high_sem, ag_sem, rs_send, up_send, down_send,
     *extra,
 ):
     z = lax.axis_index("row")
@@ -81,6 +81,8 @@
         w_copy(k).start()
         return carry
 
+    g_copy = pltpu.make_async_copy(g_hbm, g_ref, g_sem)
+    g_copy.start()
     lax.fori_loop(0, count, start_w, 0)
 
     def line_barrier():
@@ -180,41 +182,58 @@
                 if d:
                     share(dz, d).wait_send()
 
-    def sum_rows(d, which):
+    def sum_rows(t, which):
         size = dx_ref.shape[0]
-        return pl.ds(pl.multiple_of((((chip + d) % CHIPS) * CORES + which) * size, size), size)
-
-    def sum_pair(d):
-        return pltpu.make_async_remote_copy(
-            pair_out.at[d], pair_in.at[d], sum_pair_send.at[d], sum_pair_recv.at[d], **to(z, pair())
-        )
-
-    def sum_chip(d):
-        return pltpu.make_async_remote_copy(
-            chip_out.at[d], chip_in.at[d], sum_chip_send.at[d], sum_chip_recv.at[d], **to(z, other_chip(d))
-        )
-
-    def scatter_sum():
-        order = (2, 1, 3, 0)
-        for d in order:
-            pair_out[d] = dx_acc[sum_rows(d, 1 - core), :].astype(bf16)
-            sum_pair(d).start()
-        for d in order:
-            sum_pair(d).wait_recv()
-            both_cores = dx_acc[sum_rows(d, core), :] + pair_in[d].astype(f32)
-            if d:
-                chip_out[d] = both_cores.astype(bf16)
-                sum_chip(d).start()
-            else:
-                total = both_cores
-        for d in range(1, CHIPS):
-            sum_chip(d).wait_recv()
-            total += chip_in[d].astype(f32)
-        dx_ref[...] = total.astype(bf16)
-        for d in order:
-            sum_pair(d).wait_send()
-            if d:
-                sum_chip(d).wait_send()
+        return pl.ds(pl.multiple_of((t * CORES + which) * size, size), size)
+
+    def sum_pair(t):
+        return pltpu.make_async_remote_copy(
+            pair_out.at[t], pair_in.at[t], sum_pair_send.at[t], sum_pair_recv.at[t], **to(z, pair())
+        )
+
+    def sum_chip(t):
+        return pltpu.make_async_remote_copy(
+            chip_out.at[t], chip_in.at[chip], sum_chip_send.at[t], sum_chip_recv.at[chip], **to(z, t * CORES + core)
+        )
+
+    def sum_from(t):
+        return pltpu.make_async_remote_copy(
+            chip_out.at[t], chip_in.at[t], sum_chip_send.at[t], sum_chip_recv.at[t], **to(z, t * CORES + core)
+        )
+
+    def give_pair(t):
+        pair_out[t] = dx_acc[sum_rows(t, 1 - core), :].astype(bf16)
+        sum_pair(t).start()
+
+    def give_chip(t):
+        sum_pair(t).wait_recv()
+        both_cores = dx_acc[sum_rows(t, core), :] + pair_in[t].astype(f32)
+
+        @pl.when(chip != t)
+        def _():
+            chip_out[t] = both_cores.astype(bf16)
+            sum_chip(t).start()
+
+        @pl.when(chip == t)
+        def _():
+            dx_acc[sum_rows(t, core), :] = both_cores
+
+    def end_sum():
+        mine = sum_rows(chip, core)
+        for t in range(CHIPS):
+
+            @pl.when(chip != t)
+            def _():
+                sum_from(t).wait_recv()
+                dx_acc[mine, :] += chip_in[t].astype(f32)
+
+        dx_ref[...] = dx_acc[mine, :].astype(bf16)
+        for t in range(CHIPS):
+            sum_pair(t).wait_send()
+
+            @pl.when(chip != t)
+            def _():
+                sum_chip(t).wait_send()
 
     if plane:
         barrier = pltpu.get_barrier_semaphore()
@@ -230,6 +249,7 @@
 
     dx_acc[...] = jnp.zeros_like(dx_acc)
     first_matmul(0)
+    g_copy.wait()
 
     def step(s, carry):
         up_k = s - lag * z
@@ -268,7 +288,7 @@
 
                 rs_down(down_k, t).start()
 
-        own_k = s - lag * (n - 1)
+        own_k = s - lag * jnp.maximum(z, n - 1 - z)
 
         @pl.when(inside(own_k))
         def _():
@@ -302,7 +322,7 @@
                 ag_down(own_k, z).start()
 
         for t in range(n):
-            low_k = s - lag * (n - 1) - lag * (z - t)
+            low_k = s - lag * max(t, n - 1 - t) - lag * (z - t)
 
             @pl.when(both(t < z, inside(low_k)))
             def _():
@@ -312,7 +332,7 @@
                 def _():
                     ag_up(low_k, t).start()
 
-            high_k = s - lag * (n - 1) - lag * (t - z)
+            high_k = s - lag * max(t, n - 1 - t) - lag * (t - z)
 
             @pl.when(both(t > z, inside(high_k)))
             def _():
@@ -321,6 +341,25 @@
                 @pl.when(z > 0)
                 def _():
                     ag_down(high_k, t).start()
+
+        for t in range(n):
+            sum_k = s - lag * (max(t, n - 1 - t) + jnp.maximum(z - t, t - z))
+
+            @pl.when(inside(sum_k))
+            def _():
+                dx_acc[block(t), :] += lax.dot_general(
+                    hidden[sum_k, block(t)], w_v[sum_k], (((1,), (1,)), ((), ())), preferred_element_type=f32
+                )
+
+            if plane:
+
+                @pl.when(sum_k == count - 1)
+                def _():
+                    give_pair(t)
+
+                @pl.when(sum_k == count)
+                def _():
+                    give_chip(t)
 
         @pl.when(s + 1 < count)
         def _():
@@ -342,15 +381,12 @@
                 xt_ref[...], hidden[last_k], preferred_element_type=f32
             ).astype(bf16)
             dw_copy(last_k).start()
-            dx_acc[...] += lax.dot_general(
-                hidden[last_k], w_v[last_k], (((1,), (1,)), ((), ())), preferred_element_type=f32
-            )
 
         return carry
 
-    lax.fori_loop(0, count + 2 * lag * (n - 1), step, 0)
+    lax.fori_loop(0, count + 2 * lag * (n - 1) + 1, step, 0)
     if plane:
-        scatter_sum()
+        end_sum()
         end_gather()
     else:
         dx_ref[...] = dx_acc[...].astype(bf16)
@@ -410,6 +446,8 @@
         pltpu.VMEM((tokens, depth), f32),
         pltpu.VMEM((2, depth, width), bf16),
         pltpu.VMEM((depth, tokens), bf16),
+        pltpu.VMEM((rows, units), bf16),
+        dma,
         dma((count,)),
         dma((2,)),
     ] + [dma((count, n))] * 6
@@ -429,7 +467,7 @@
             jax.ShapeDtypeStruct((sum_rows, depth), bf16),
             jax.ShapeDtypeStruct((depth, units), bf16),
         ),
-        in_specs=[vmem, hbm, vmem],
+        in_specs=[vmem, hbm, hbm],
         out_specs=(vmem, vmem, hbm),
         scratch_shapes=scratch,
         compiler_params=pltpu.CompilerParams(

time: 137 us -> 133 us (0.971)
  the two profiles are of different devices: /device:TPU:0 before, /device:TPU:7 now
where the time goes in v4:
time: 133 us; the launch traced here: 132 us
  Pallas kernels  120 us (90%)
  local copies, waits for them, and re-layouts  11.9 us (9%)
    pallas_call x1, Pallas kernels, grid_call(): pl.pallas_call(functools.partial(grid_kernel, n, count, width, rows, LAG,...  120 us
    unnamed x3, local copies, waits for them, and re-layouts  11.9 us

profile of v4, /device:TPU:7, one launch (start us, length us, event | category | flops | bytes accessed | tf_op | source)
XLA Modules:
  0.0 132.5 jit_solution(13182582516077043531)
XLA Ops:
  0.6 119.9 %shard_map.58 = (bf16[128,3072]{1,0:T(8,128)(2,1)}, bf16[64,1536]{1,0:T(8,128)(2,1)}, bf16[1536,3072]{1,0:T(8,128)(2,1)}) custom-call(bf16[128,768]{1,0:T(8,128)(2,1)} %x_in.1, bf16[1536,3072]{1,0:T(8,128)(2,1)} %w_hbm.1, bf16[128,3072]{1,0:T(8,128)(2,1)} %g_hbm.1), custom_call_target="tpu_custom_call" | custom-call | flops 14495514624 | bytes 18874368 | tf_op jit(solution)/shard_map/pallas_call | solution.py:463
  120.5 2.1 %copy.9 = bf16[128,3072]{1,0:T(8,128)(2,1)} copy(bf16[128,3072]{1,0:T(8,128)(2,1)} %get-tuple-element.6) | data formatting | bytes 1572864
  122.6 1.6 %copy.10 = bf16[64,1536]{1,0:T(8,128)(2,1)} copy(bf16[64,1536]{1,0:T(8,128)(2,1)} %get-tuple-element.7) | data formatting | bytes 393216
  124.2 8.3 %copy.11 = bf16[1536,3072]{1,0:T(8,128)(2,1)} copy(bf16[1536,3072]{1,0:T(8,128)(2,1)} %get-tuple-element.8) | data formatting | bytes 18874368

commit v5 on v4

--- a/solution.py
+++ b/solution.py
@@ -47,7 +47,7 @@
         return pltpu.make_async_copy(dw_v.at[lax.rem(k, 2)], dw_hbm.at[:, cols], dw_sem.at[lax.rem(k, 2)])
 
     def block(t):
-        return pl.ds(t * rows, rows)
+        return pl.ds(t * rows if isinstance(t, int) else pl.multiple_of(t * rows, rows), rows)
 
     def send_up(src, dst, send, recv):
         return pltpu.make_async_remote_copy(src, dst, send, recv, device_id={"row": z + 1}, device_id_type=pl.DeviceIdType.MESH)
@@ -167,9 +167,28 @@
             for d in (1, 3, 2):
                 share(dz, d).wait_recv()
                 to_pair(dz, d).start()
-        for dz in range(n):
-            for d in range(CHIPS):
-                to_pair(dz, d).wait_recv()
+            if dz:
+                begin(dz - 1)
+        begin(n - 1)
+
+    def begin(dz):
+        for d in range(CHIPS):
+            to_pair(dz, d).wait_recv()
+        if dz == 0:
+            w_copy(0).wait()
+        t = (z - dz + n) % n
+        p_v[0, block(t)] = jnp.dot(x_ref[block(t), :], w_v[0], preferred_element_type=f32)
+        if dz:
+
+            @pl.when(z == 0)
+            def _():
+                stage[0, block(t)] = p_v[0, block(t)].astype(bf16)
+                rs_up(0, t).start()
+
+            @pl.when(z == n - 1)
+            def _():
+                stage[0, block(t)] = p_v[0, block(t)].astype(bf16)
+                rs_down(0, t).start()
 
     def end_gather():
         for d in range(1, CHIPS):
@@ -248,14 +267,17 @@
         line_barrier()
 
     dx_acc[...] = jnp.zeros_like(dx_acc)
-    first_matmul(0)
+    if not plane:
+        first_matmul(0)
     g_copy.wait()
+
+    begun = 1 if plane else 0
 
     def step(s, carry):
         up_k = s - lag * z
         for t in range(n - 1, 0, -1):
 
-            @pl.when(both(t > z, inside(up_k)))
+            @pl.when(both(both(t > z, inside(up_k)), jnp.logical_or(z > 0, up_k >= begun)))
             def _():
                 @pl.when(z > 0)
                 def _():
@@ -273,7 +295,7 @@
         down_k = s - lag * (n - 1 - z)
         for t in range(n - 1):
 
-            @pl.when(both(t < z, inside(down_k)))
+            @pl.when(both(both(t < z, inside(down_k)), jnp.logical_or(z < n - 1, down_k >= begun)))
             def _():
                 @pl.when(z < n - 1)
                 def _():

time: 133 us -> 130 us (0.977)
  Pallas kernels: 120 us -> 118 us
    pallas_call x1, Pallas kernels: 120 us -> 118 us  [grid_call(): pl.pallas_call(functools.partial(grid_kernel, n, count, width, rows, LAG,...]
where the time goes in v5:
time: 130 us
  Pallas kernels  118 us (91%)
  local copies, waits for them, and re-layouts  11.9 us (9%)
    pallas_call x1, Pallas kernels, grid_call(): pl.pallas_call(functools.partial(grid_kernel, n, count, width, rows, LAG,...  118 us
    unnamed x3, local copies, waits for them, and re-layouts  11.9 us

profile of v5, /device:TPU:7, one launch (start us, length us, event | category | flops | bytes accessed | tf_op | source)
XLA Modules:
  0.0 130.2 jit_solution(6211847658235059135)
XLA Ops:
  0.6 117.6 %shard_map.58 = (bf16[128,3072]{1,0:T(8,128)(2,1)}, bf16[64,1536]{1,0:T(8,128)(2,1)}, bf16[1536,3072]{1,0:T(8,128)(2,1)}) custom-call(bf16[128,768]{1,0:T(8,128)(2,1)} %x_in.1, bf16[1536,3072]{1,0:T(8,128)(2,1)} %w_hbm.1, bf16[128,3072]{1,0:T(8,128)(2,1)} %g_hbm.1), custom_call_target="tpu_custom_call" | custom-call | flops 14495514624 | bytes 18874368 | tf_op jit(solution)/shard_map/pallas_call | solution.py:485
  118.3 2.1 %copy.9 = bf16[128,3072]{1,0:T(8,128)(2,1)} copy(bf16[128,3072]{1,0:T(8,128)(2,1)} %get-tuple-element.6) | data formatting | bytes 1572864
  120.3 1.6 %copy.10 = bf16[64,1536]{1,0:T(8,128)(2,1)} copy(bf16[64,1536]{1,0:T(8,128)(2,1)} %get-tuple-element.7) | data formatting | bytes 393216
  121.9 8.3 %copy.11 = bf16[1536,3072]{1,0:T(8,128)(2,1)} copy(bf16[1536,3072]{1,0:T(8,128)(2,1)} %get-tuple-element.8) | data formatting | bytes 18874368
